TPU v7x, 32 devices: a whole 2x2x4 slice. The times are simulated.
32 devices in a mesh: gx: 4 (over z), gy: 8 (over y, x, core).
Axes of the slice: x: 2, y: 2, z: 4, core: 2. Of those that a mesh axis runs over, the one named last changes fastest.
Arguments:
- tokens: bfloat16 [256, 14, 20, 384], P(('gx', 'gy')), may hold values from -6 to 6
- bucket: int32 [256], P(('gx', 'gy')), may hold values from 0 to 1
- counts: int32 [32], P(('gx', 'gy')), may hold values from 4 to 8, as said below
- mod_weights: bfloat16 [591360], P(('gx', 'gy')), may hold values from -0.3125 to 0.3125
- mlp_weights: bfloat16 [1179648], P(('gx', 'gy')), may hold values from -0.3125 to 0.3125
- small_params: bfloat16 [37664], P(('gx', 'gy')), as said below
- cotangent: bfloat16 [256, 14, 20, 384], P(('gx', 'gy')), may hold values from -6 to 6
Outputs:
- out_tokens: bfloat16 [256, 14, 20, 384], P(('gx', 'gy'))
- grad_tokens: float32 [256, 14, 20, 384], P(('gx', 'gy'))
- grad_mod: float32 [591360], P(('gx', 'gy'))
- grad_mlp: float32 [1179648], P(('gx', 'gy'))
- grad_small: float32 [37664], P(('gx', 'gy'))
Inputs may be any that keep to these rules, and one draw needn't show every extreme that they name: `counts`: each device's live slots; some device holds exactly 8. `small_params`: Gains, biases, depthwise kernels and layer scales in the stated layout.
All inputs are finite; a program needn't handle non-finite values.
Results may differ from a plain program's by a relative error of at most 0.0084.
Values may be sent and summed in bfloat16 or wider, within the bound.
No kernel may reach another device: no remote copies, remote signals or barrier semaphores. Data moves between devices by JAX's collectives and lax.ppermute only.
A program may use at most 448 MiB of HBM per device.

v0:
```python
import jax
import jax.numpy as jnp
from jax import lax
from jax.sharding import PartitionSpec as P

C = 384
HID = 1536


epsilon = 1e-05


def matmul(left, right):
    return jnp.dot(left, right, preferred_element_type=jnp.float32)


def outer_sum(left, right):
    return lax.dot_general(
        left, right, (((0,), (0,)), ((), ())), preferred_element_type=jnp.float32
    )


def times_turned(left, right):
    return lax.dot_general(
        left, right, (((1,), (1,)), ((), ())), preferred_element_type=jnp.float32
    )


def column_sums(values):
    return jnp.sum(values.astype(jnp.float32), axis=0)


def gelu_exact(values):
    return jax.nn.gelu(values, approximate=False)


def layer_norm(field_in, gain_vec, shift_vec):
    average = jnp.mean(field_in, axis=-1, keepdims=True)
    centred = field_in - average
    variance = jnp.mean(centred * centred, axis=-1, keepdims=True)
    return centred * lax.rsqrt(variance + epsilon) * gain_vec + shift_vec


def depthwise(field_in, kernel):
    kernel_width = kernel.shape[1]
    half_width = kernel_width // 2
    padded = jnp.pad(field_in, ((0, 0), (half_width, half_width), (half_width, half_width), (0, 0)))
    rows_in = field_in.shape[1]
    cols_in = field_in.shape[2]
    ctx_total = jnp.zeros_like(field_in)
    for row_shift in range(kernel_width):
        for col_shift in range(kernel_width):
            window = padded[:, row_shift : row_shift + rows_in, col_shift : col_shift + cols_in, :]
            ctx_total = ctx_total + window * kernel[:, row_shift, col_shift][:, None, None, :]
    return ctx_total


def oriented(kernel, bucket):
    turned = jnp.swapaxes(kernel, 0, 1)
    turned_mask = (bucket == 1)[:, None, None, None]
    return jnp.where(turned_mask, turned[None], kernel[None])


def focal(context, gates, bucket, kernels):
    level_ctx = context
    ctx_total = jnp.zeros_like(context)
    for level_index in range(3):
        level_ctx = gelu_exact(depthwise(level_ctx, oriented(kernels[level_index], bucket)))
        ctx_total = ctx_total + level_ctx * gates[..., level_index : level_index + 1]
    summary = gelu_exact(jnp.mean(level_ctx, axis=(1, 2), keepdims=True))
    return ctx_total + summary * gates[..., 3:4]


def unpack_small(small_vec):
    lengths = [C, C, 2 * C + 4, 9 * C, 25 * C, 49 * C, C, C, C, C, C, HID, C, C]
    pieces = []
    offset = 0
    for length in lengths:
        pieces.append(small_vec[offset : offset + length])
        offset = offset + length
    kernels = (pieces[3].reshape(3, 3, C), pieces[4].reshape(5, 5, C), pieces[5].reshape(7, 7, C))
    return (
        pieces[0],
        pieces[1],
        pieces[2],
        kernels,
        pieces[6],
        pieces[7],
        pieces[8],
        pieces[9],
        pieces[10],
        pieces[11],
        pieces[12],
        pieces[13],
    )


def split_mod(flat_vec):
    boundary = C * (2 * C + 4)
    return (
        flat_vec[:boundary].reshape(C, 2 * C + 4),
        flat_vec[boundary : boundary + C * C].reshape(C, C),
        flat_vec[boundary + C * C :].reshape(C, C),
    )


def split_mlp(flat_vec):
    return (flat_vec[: C * HID].reshape(C, HID), flat_vec[C * HID :].reshape(HID, C))


def local(tokens, bucket, counts, mod_weights, mlp_weights, small_params, cotangent):
    mod_full, small_full = (
        lax.all_gather(mod_weights, ("gx", "gy"), axis=0, tiled=True),
        lax.all_gather(small_params, ("gx", "gy"), axis=0, tiled=True),
    )
    mlp_full = lax.all_gather(mlp_weights, ("gx", "gy"), axis=0, tiled=True)
    small32 = small_full.astype(jnp.float32)
    (
        gain_one,
        shift_one,
        merged_bias,
        kernels,
        mod_bias,
        proj_bias,
        scale_one,
        gain_two,
        shift_two,
        up_bias,
        down_bias,
        scale_two,
    ) = unpack_small(small32)
    w_merged, w_modul, w_proj = split_mod(mod_full)
    w_up, w_down = split_mlp(mlp_full)
    grid_shape = tokens.shape
    slot_count = grid_shape[0]
    live_mask = (jnp.arange(slot_count, dtype=jnp.int32) < counts[0]).astype(jnp.float32)
    rows_alive = jnp.broadcast_to(
        live_mask[:, None], (slot_count, grid_shape[1] * grid_shape[2])
    ).reshape(-1, 1)
    flat_in = tokens.reshape(-1, C).astype(jnp.float32)
    normed32, first_pull = jax.vjp(layer_norm, flat_in, gain_one, shift_one)
    normed = normed32.astype(jnp.bfloat16)
    merged_out = matmul(normed, w_merged) + merged_bias
    query_part = merged_out[:, :C]

    def context_piece(ctx_gates, kernel_set):
        context = ctx_gates[:, :C].reshape(grid_shape)
        gates = ctx_gates[:, C:].reshape(grid_shape[:3] + (4,))
        return focal(context, gates, bucket, kernel_set).reshape(-1, C)

    mixed32, focal_pull = jax.vjp(context_piece, merged_out[:, C:], kernels)
    mixed_ctx = mixed32.astype(jnp.bfloat16)
    modulator = matmul(mixed_ctx, w_modul) + mod_bias
    modulated = (query_part * modulator).astype(jnp.bfloat16)
    branch = matmul(modulated, w_proj) + proj_bias
    middle = flat_in + scale_one * branch
    second32, second_pull = jax.vjp(layer_norm, middle, gain_two, shift_two)
    second = second32.astype(jnp.bfloat16)
    expanded = matmul(second, w_up) + up_bias
    activated32, gelu_pull = jax.vjp(gelu_exact, expanded)
    activated = activated32.astype(jnp.bfloat16)
    shrunk = matmul(activated, w_down) + down_bias
    result = (middle + scale_two * shrunk) * rows_alive
    out_tokens = result.reshape(grid_shape).astype(jnp.bfloat16)
    mlp_again = lax.all_gather(mlp_weights, ("gx", "gy"), axis=0, tiled=True)
    up_back, down_back = split_mlp(mlp_again)
    upstream = cotangent.reshape(-1, C).astype(jnp.float32) * rows_alive
    d_shrunk = (upstream * scale_two).astype(jnp.bfloat16)
    grad_scale_two = jnp.sum(upstream * shrunk, axis=0)
    grad_down_bias = column_sums(d_shrunk)
    grad_down = outer_sum(activated, d_shrunk)
    d_activated = times_turned(d_shrunk, down_back)
    (d_expanded32,) = gelu_pull(d_activated)
    d_expanded = d_expanded32.astype(jnp.bfloat16)
    grad_up_bias = column_sums(d_expanded)
    grad_up = outer_sum(second, d_expanded)
    d_second = times_turned(d_expanded, up_back)
    d_middle_part, grad_gain_two, grad_shift_two = second_pull(d_second)
    d_middle = upstream + d_middle_part
    mlp_grad_flat = jnp.concatenate([grad_up.reshape(-1), grad_down.reshape(-1)])
    grad_mlp = lax.psum_scatter(mlp_grad_flat, ("gx", "gy"), scatter_dimension=0, tiled=True)
    mod_again = lax.all_gather(mod_weights, ("gx", "gy"), axis=0, tiled=True)
    merged_back, modul_back, proj_back = split_mod(mod_again)
    d_branch = (d_middle * scale_one).astype(jnp.bfloat16)
    grad_scale_one = jnp.sum(d_middle * branch, axis=0)
    grad_proj_bias = column_sums(d_branch)
    grad_proj = outer_sum(modulated, d_branch)
    d_modulated = times_turned(d_branch, proj_back)
    d_query = d_modulated * modulator
    d_modulator = (d_modulated * query_part).astype(jnp.bfloat16)
    grad_mod_bias = column_sums(d_modulator)
    grad_modul = outer_sum(mixed_ctx, d_modulator)
    d_mixed = times_turned(d_modulator, modul_back)
    d_ctx_gates, kernel_grads = focal_pull(d_mixed)
    d_merged = jnp.concatenate([d_query, d_ctx_gates], axis=1).astype(jnp.bfloat16)
    grad_merged_bias = column_sums(d_merged)
    grad_merged = outer_sum(normed, d_merged)
    d_normed = times_turned(d_merged, merged_back)
    d_input_part, grad_gain_one, grad_shift_one = first_pull(d_normed)
    grad_tokens = (d_middle + d_input_part).reshape(grid_shape)
    used_small = 94 * C + 4 + HID
    padding = jnp.zeros((small_full.shape[0] - used_small,), jnp.float32)
    small_grad_flat = jnp.concatenate(
        [
            grad_gain_one,
            grad_shift_one,
            grad_merged_bias,
            kernel_grads[0].reshape(-1),
            kernel_grads[1].reshape(-1),
            kernel_grads[2].reshape(-1),
            grad_mod_bias,
            grad_proj_bias,
            grad_scale_one,
            grad_gain_two,
            grad_shift_two,
            grad_up_bias,
            grad_down_bias,
            grad_scale_two,
            padding,
        ]
    )
    mod_grad_flat = jnp.concatenate(
        [grad_merged.reshape(-1), grad_modul.reshape(-1), grad_proj.reshape(-1)]
    )
    grad_mod, grad_small = (
        lax.psum_scatter(mod_grad_flat, ("gx", "gy"), scatter_dimension=0, tiled=True),
        lax.psum_scatter(small_grad_flat, ("gx", "gy"), scatter_dimension=0, tiled=True),
    )
    return (out_tokens, grad_tokens, grad_mod, grad_mlp, grad_small)


def solution(mesh):
    return jax.shard_map(
        local,
        mesh=mesh,
        in_specs=(
            P(("gx", "gy"), None, None, None),
            P(("gx", "gy")),
            P(("gx", "gy")),
            P(("gx", "gy")),
            P(("gx", "gy")),
            P(("gx", "gy")),
            P(("gx", "gy"), None, None, None),
        ),
        out_specs=(
            P(("gx", "gy"), None, None, None),
            P(("gx", "gy"), None, None, None),
            P(("gx", "gy")),
            P(("gx", "gy")),
            P(("gx", "gy")),
        ),
        check_vma=False,
    )
```

profile of v0, /device:TPU:0, one launch (start us, length us, event | category | flops | bytes accessed | tf_op | source)
XLA Modules:
  0.0 1047.7 jit_solution(3025536789949164190)
XLA Ops:
  27.2 4.9 reshape.939
  32.0 4.7 reshape.938
  36.7 111.0 %all-reduce.187.cloned.1.call-done = (bf16[37664]{0:T(1024)(128)(2,1)}, bf16[591360]{0:T(1024)(128)(2,1)}) async-done(((bf16[37664]{0:T(1024)(128)(2,1)}, bf16[591360]{0:T(1024)(128)(2,1)}), (bf16[37664]{0:T(1024)(128)(2,1)}, bf16[591360]{0:T(1024)(128)(2,1)})) %all-reduce.187.cloned.1.call-update) | async-done | bytes 1258064
  162.2 3.6 convolution_add_fusion.1
  165.8 2.9 copy-done.8
  168.9 3.1 copy.94
  172.1 4.7 reshape.835
  177.1 26.2 %multiply_multiply_fusion.22 = (f32[8,14,20,384]{3,2,1,0:T(8,128)S(1)}, f32[8,14,20,384]{3,2,1,0:T(8,128)}) fusion(f32[8,384]{1,0:T(8,128)S(1)} %copy-done.48, f32[8,384]{1,0:T(8,128)S(1)} %copy-done.50, f32[8,384]{1,0:T(8,128)S(1)} %copy-done.52, f32[8,384]{1,0:T(8,128)S(1)} %copy-done.54, f32[8,14,20,384]{3,2,1,0:T(8,128)} %reshape.835, ...), kind=kLoop, calls=%fused_computation.272 | loop fusion | flops 69672960 | bytes 10432512 | tf_op jit(solution)/shard_map/jvp()/mul | solution.py:34
  203.7 25.7 %multiply_multiply_fusion.21 = (f32[8,14,20,384]{3,2,1,0:T(8,128)S(1)}, f32[8,14,20,384]{3,2,1,0:T(8,128)}) fusion(f32[8,384]{1,0:T(8,128)S(1)} %copy-done.106, f32[8,384]{1,0:T(8,128)S(1)} %copy-done.108, f32[8,384]{1,0:T(8,128)S(1)} %copy-done.110, f32[8,384]{1,0:T(8,128)S(1)} %copy-done.112, f32[8,384]{1,0:T(8,128)S(1)} %copy-done.114, ...), kind=kLoop, calls=%fused_computation.271 | loop fusion | flops 97198080 | bytes 10629120 | tf_op jit(solution)/shard_map/jvp()/mul | solution.py:34
  229.6 50.3 %fusion.45 = (f32[8,384]{1,0:T(8,128)S(1)}, f32[8,14,20,384]{3,2,1,0:T(8,128)}, f32[8,14,20,384]{3,2,1,0:T(8,128)}) fusion(f32[8,384]{1,0:T(8,128)S(1)} %copy-done.146, f32[8,384]{1,0:T(8,128)} %get-tuple-element.252, f32[8,384]{1,0:T(8,128)} %get-tuple-element.253, f32[8,384]{1,0:T(8,128)} %get-tuple-element.254, f32[8,384]{1,0:T(8,128)} %get-tuple-element.255, ...), kind=kLoop, calls=%fused_computation.531 | loop fusion | flops 139342848 | bytes 10936320 | tf_op jit(solution)/shard_map/jvp()/reduce_sum | solution.py:70
  285.2 6.6 add_convert_fusion.1
  293.7 5.8 multiply_convert_fusion.3
  299.6 3.2 fusion.50
  311.1 36.5 %multiply_convert_fusion = (bf16[2240,1536]{1,0:T(8,128)(2,1)}, f32[2240,1536]{1,0:T(8,128)}, f32[2240,1536]{1,0:T(8,128)}) fusion(f32[1536]{0:T(1024)} %slice.920, bf16[384,1536]{1,0:T(8,128)(2,1)S(1)} %slice.809, f32[2240,384]{1,0:T(8,128)} %copy-done.12, f32[384]{0:T(512)} %get-tuple-element.342, f32[384]{0:T(512)S(1)} %copy-done.221, f32[2240]{0:T(1024)} %fusion.40, ...), kind=kOutput, calls=%fused_computation.53 | convolution fusion | flops 2873794560 | bytes 39053824 | tf_op jit(solution)/shard_map/dot_general | solution.py:14
  347.7 16.7 %convert_reduce_fusion = (f32[1536]{0:T(1024)}, bf16[2240,1536]{1,0:T(8,128)(2,1)}) fusion(f32[2240,1536]{1,0:T(8,128)} %get-tuple-element.148, f32[2240,1536]{1,0:T(8,128)} %get-tuple-element.351, bf16[1536,384]{1,0:T(8,128)(2,1)S(1)} %slice.812, f32[2240,384]{1,0:T(8,128)S(1)} %copy-done.10, f32[2240]{0:T(1024)S(1)} %copy-done.187, f32[384]{0:T(512)S(1)} %copy-done.215), kind=kOutput, calls=%fused_computation.51 | convolution fusion | flops 2700040704 | bytes 39043328 | tf_op jit(solution)/shard_map/dot_general | solution.py:24
  364.4 10.7 %multiply_reduce_fusion.89 = (f32[384]{0:T(512)}, f32[2240]{0:T(1024)S(1)}, f32[384]{0:T(512)}, f32[2240,384]{1,0:T(8,128)}) fusion(f32[2240,384]{1,0:T(8,128)} %copy-done.12, f32[2240]{0:T(1024)S(1)} %copy-done.206, f32[2240]{0:T(1024)S(1)} %copy-done.189, f32[384]{0:T(512)S(1)} %copy-done.221, bf16[2240,1536]{1,0:T(8,128)(2,1)} %get-tuple-element.358, ...), kind=kOutput, calls=%fused_computation.282 | convolution fusion | flops 2649289728 | bytes 14973696 | tf_op jit(solution)/shard_map/dot_general | solution.py:24
  375.1 4.6 fusion.46
  379.8 5.6 fusion.44
  385.4 9.1 fusion.48
  401.3 3.2 convert_reduce_fusion.2
  411.1 3.7 multiply_reduce_fusion.83
  414.8 40.1 %multiply_reduce_fusion.47 = (f32[8,384]{1,0:T(8,128)}, f32[8,384]{1,0:T(8,128)}, f32[8,384]{1,0:T(8,128)}, f32[8,384]{1,0:T(8,128)}, f32[8,384]{1,0:T(8,128)}, ...) fusion(f32[8,14,20,384]{3,2,1,0:T(8,128)} %copy-done, ...), kind=kLoop, calls=%fused_computation.183 | loop fusion | flops 43812864 | bytes 17445632 | tf_op jit(solution)/shard_map/transpose(jvp())/reduce_sum | solution.py:54
  454.9 25.7 %multiply_reduce_fusion.46 = (f32[8,384]{1,0:T(8,128)}, f32[8,384]{1,0:T(8,128)}, f32[8,384]{1,0:T(8,128)}, f32[8,384]{1,0:T(8,128)}, f32[8,384]{1,0:T(8,128)}, ...) fusion(f32[8,14,20,384]{3,2,1,0:T(8,128)} %get-tuple-element.14, ...), kind=kLoop, calls=%fused_computation.182 | loop fusion | flops 29198784 | bytes 17402112 | tf_op jit(solution)/shard_map/transpose(jvp())/reduce_sum | solution.py:54
  480.7 28.1 %multiply_reduce_fusion.48 = (f32[8,384]{1,0:T(8,128)}, f32[8,384]{1,0:T(8,128)}, f32[8,384]{1,0:T(8,128)}, f32[8,384]{1,0:T(8,128)}, f32[8,384]{1,0:T(8,128)}, ...) fusion(f32[8,14,20,384]{3,2,1,0:T(8,128)} %get-tuple-element.14, ...), kind=kLoop, calls=%fused_computation.184 | loop fusion | flops 30910464 | bytes 7102464 | tf_op jit(solution)/shard_map/transpose(jvp())/reduce_sum | solution.py:54
  509.1 18.6 %broadcast_multiply_fusion.2 = (f32[8,14,20,384]{3,2,1,0:T(8,128)}, f32[8,14,20,384]{3,2,1,0:T(8,128)}, f32[8,14,20,384]{3,2,1,0:T(8,128)}, f32[8,14,20,384]{3,2...) fusion(f32[8,14,20,384]{3,2,1,0:T(8,128)} %get-tuple-element.14, ...), kind=kLoop, calls=%fused_computation.303 | loop fusion | flops 11182080 | bytes 48328704 | tf_op jit(solution)/shard_map/transpose(jvp())/mul | solution.py:54
  528.0 25.2 %broadcast_multiply_fusion.1 = (f32[8,14,20,384]{3,2,1,0:T(8,128)}, f32[8,14,20,384]{3,2,1,0:T(8,128)}, f32[8,14,20,384]{3,2,1,0:T(8,128)}, f32[8,14,20,384]{3,2...) fusion(f32[8,14,20,384]{3,2,1,0:T(8,128)} %get-tuple-element.14, ...), kind=kLoop, calls=%fused_computation.302 | loop fusion | flops 15482880 | bytes 65593344 | tf_op jit(solution)/shard_map/transpose(jvp())/mul | solution.py:54
  553.4 25.1 %broadcast_multiply_fusion = (f32[8,14,20,384]{3,2,1,0:T(8,128)}, f32[8,14,20,384]{3,2,1,0:T(8,128)}, f32[8,14,20,384]{3,2,1,0:T(8,128)}, f32[8,14,20,384]{3,2,1...) fusion(f32[8,14,20,384]{3,2,1,0:T(8,128)} %get-tuple-element.14, ...), kind=kLoop, calls=%fused_computation.301 | loop fusion | flops 15482880 | bytes 65593344 | tf_op jit(solution)/shard_map/transpose(jvp())/mul | solution.py:54
  578.6 59.7 %pad_add_fusion = f32[8,20,26,384]{3,2,1,0:T(8,128)} fusion(f32[8,14,20,384]{3,2,1,0:T(8,128)} %get-tuple-element.201, f32[8,14,20,384]{3,2,1,0:T(8,128)} %get-tuple-element.202, f32[8,14,20,384]{3,2,1,0:T(8,128)} %get-tuple-element.203, f32[8,14,20,384]{3,2,1,0:T(8,128)} %get-tuple-element.204, f32[8,14,20,384]{3,2,1,0:T(8,128)} %get-tuple-element.205, ...), kind=kLoop, calls=%fused_computation.91 | loop fusion | flops 67092480 | bytes 154337280 | tf_op jit(solution)/shard_map/transpose(jvp())/add_any | solution.py:53
  638.3 46.6 %multiply_reduce_fusion.73 = (f32[8,384]{1,0:T(8,128)}, f32[8,384]{1,0:T(8,128)}, f32[8,384]{1,0:T(8,128)}, f32[8,384]{1,0:T(8,128)}, f32[8,384]{1,0:T(8,128)}, ...) fusion(f32[8,14,20,384]{3,2,1,0:T(8,128)} %copy-done.2, ...), kind=kLoop, calls=%fused_computation.209 | loop fusion | flops 98863104 | bytes 38077184 | tf_op jit(solution)/shard_map/transpose(jvp())/reduce_sum | solution.py:54
  685.1 27.2 %multiply_reduce_fusion.72 = (f32[8,384]{1,0:T(8,128)S(1)}, f32[8,384]{1,0:T(8,128)S(1)}, f32[8,384]{1,0:T(8,128)}, f32[8,384]{1,0:T(8,128)}, f32[8,384]{1,0:T(8...) fusion(f32[8,14,20,384]{3,2,1,0:T(8,128)} %get-tuple-element.14, ...), kind=kLoop, calls=%fused_computation.208 | loop fusion | flops 21480256 | bytes 41493248 | tf_op jit(solution)/shard_map/transpose(jvp())/reduce_sum | solution.py:54
  712.5 22.7 %broadcast_multiply_fusion.49 = (f32[8,14,20,384]{3,2,1,0:T(8,128)}, f32[8,14,20,384]{3,2,1,0:T(8,128)}, f32[8,14,20,384]{3,2,1,0:T(8,128)}, f32[8,14,20,384]{3,...) fusion(f32[8,14,20,384]{3,2,1,0:T(8,128)} %get-tuple-element.14, ...), kind=kLoop, calls=%fused_computation.350 | loop fusion | flops 13762560 | bytes 58687488 | tf_op jit(solution)/shard_map/transpose(jvp())/mul | solution.py:54
  735.7 28.5 %pad_add_fusion.1 = f32[8,18,24,384]{3,2,1,0:T(8,128)} fusion(f32[8,14,20,384]{3,2,1,0:T(8,128)} %get-tuple-element.166, f32[8,14,20,384]{3,2,1,0:T(8,128)} %get-tuple-element.167, f32[8,14,20,384]{3,2,1,0:T(8,128)} %get-tuple-element.168, f32[8,14,20,384]{3,2,1,0:T(8,128)} %get-tuple-element.179, f32[8,14,20,384]{3,2,1,0:T(8,128)} %get-tuple-element.180, ...), kind=kLoop, calls=%fused_computation.97 | loop fusion | flops 23887872 | bytes 70680576 | tf_op jit(solution)/shard_map/transpose(jvp())/add_any | solution.py:53
  764.3 33.7 %multiply_reduce_fusion.82 = (f32[8,384]{1,0:T(8,128)}, f32[8,384]{1,0:T(8,128)}, f32[8,384]{1,0:T(8,128)}, f32[8,384]{1,0:T(8,128)}, f32[8,384]{1,0:T(8,128)}, ...) fusion(f32[8,14,20,384]{3,2,1,0:T(8,128)} %reshape.835, ...), kind=kLoop, calls=%fused_computation.218 | loop fusion | flops 83407872 | bytes 37966592 | tf_op jit(solution)/shard_map/transpose(jvp())/reduce_sum | solution.py:54
  798.1 9.5 broadcast_multiply_fusion.74
  807.7 3.2 pad_add_fusion.2
  810.8 11.3 %pad_add_fusion.3 = f32[8,14,20,384]{3,2,1,0:T(8,128)} fusion(f32[8,14,20,384]{3,2,1,0:T(8,128)} %get-tuple-element.170, f32[8,14,20,384]{3,2,1,0:T(8,128)} %get-tuple-element.171, f32[8,14,20,384]{3,2,1,0:T(8,128)} %get-tuple-element.172, f32[8,14,20,384]{3,2,1,0:T(8,128)} %get-tuple-element.173, f32[8,14,20,384]{3,2,1,0:T(8,128)} %get-tuple-element.174, ...), kind=kLoop, calls=%fused_computation.116 | loop fusion | flops 5160960 | bytes 27525120 | tf_op jit(solution)/shard_map/transpose(jvp())/add_any | solution.py:53
  822.2 2.9 reshape.845
  825.1 3.2 copy.108
  832.0 3.8 fusion.26
  835.8 6.2 multiply_reduce_fusion.91
  842.1 3.2 reshape.850
  845.3 3.3 reshape.851
  857.6 3.3 reshape.847
  860.8 4.5 pad_maximum_fusion
  869.1 3.7 convert_element_type.110
  872.8 3.4 copy.115
  881.5 5.2 copy.116
  886.6 149.5 %all-reduce.185.cloned.1.call-done = (f32[591360]{0:T(1024)}, f32[1179648]{0:T(1024)}, f32[37664]{0:T(1024)}) async-done(((f32[591360]{0:T(1024)}, f32[1179648]{0:T(1024)}, f32[37664]{0:T(1024)}), (f32[591360]{0:T(1024)}, f32[1179648]{0:T(1024)}, f32[37664]{0:T(1024)})) %all-reduce.185.cloned.1.call-update) | async-done | bytes 7234704
  (564 shorter events, 89.4 us)
Async XLA Ops:
  7.2 140.5 %all-reduce.187.cloned.1.call-start = ((), (), s32[]{:S(2)}) async-start(), calls=%async_computation.2 | async-start | bytes 2519040
  10.6 296.7 %all-gather.2.cloned.1.call-start = ((), (), s32[]{:S(2)}) async-start(), calls=%async_computation | async-start | bytes 2433024 | tf_op jit(solution)/shard_map/all_gather | solution.py:116
  11.3 1024.9 %all-reduce.185.cloned.1.call-start = ((), (), s32[]{:S(2)}) async-start(), calls=%async_computation.1 | async-start | bytes 14475264
  20.0 136.2 %copy-start.200 = (pred[8]{0:T(512)(128)(4,1)}, pred[8]{0:T(512)(128)(4,1)S(1)}, u32[]{:S(2)}) copy-start(pred[8]{0:T(512)(128)(4,1)S(1)} %broadcast_compare_fusion) | copy-start | bytes 28
  36.7 122.9 %copy-start.24 = (f32[8,14,20]{0,2,1:T(8,128)S(1)}, f32[8,14,20]{0,2,1:T(8,128)}, u32[]{:S(2)}) copy-start(f32[8,14,20]{0,2,1:T(8,128)} %copy-done.23) | copy-start | bytes 26884
  36.7 123.0 %copy-start.30 = (f32[8,14,20]{0,2,1:T(8,128)S(1)}, f32[8,14,20]{0,2,1:T(8,128)}, u32[]{:S(2)}) copy-start(f32[8,14,20]{0,2,1:T(8,128)} %get-tuple-element.329) | copy-start | bytes 26884
  150.7 148.9 %copy-start.198 = (f32[384]{0:T(512)}, f32[384]{0:T(512)S(1)}, u32[]{:S(2)}) copy-start(f32[384]{0:T(512)S(1)} %get-tuple-element.343) | copy-start | bytes 4612
  229.4 50.5 %copy-start = (f32[8,14,20,384]{3,2,1,0:T(8,128)}, f32[8,14,20,384]{3,2,1,0:T(8,128)S(1)}, u32[]{:S(2)}) copy-start(f32[8,14,20,384]{3,2,1,0:T(8,128)S(1)} %get-tuple-element.156) | copy-start | bytes 10321924
  229.6 54.1 %slice-start.2 = ((f32[2240,772]{0,1:T(8,128)}), f32[2240,4]{0,1:T(4,128)S(1)}, s32[]{:S(2)}) async-start(f32[2240,772]{0,1:T(8,128)} %copy-done.8), calls=%async_computation.5 | async-start | bytes 73728 | tf_op jit(solution)/shard_map/jvp()/slice | solution.py:148
  311.0 36.6 %copy-start.10 = (f32[2240,384]{1,0:T(8,128)S(1)}, f32[2240,384]{1,0:T(8,128)}, u32[]{:S(2)}) copy-start(f32[2240,384]{1,0:T(8,128)} %reshape.939) | copy-start | bytes 10321924
  311.1 36.6 %copy-start.187 = (f32[2240]{0:T(1024)S(1)}, f32[2240]{0:T(1024)}, u32[]{:S(2)}) copy-start(f32[2240]{0:T(1024)} %mul.2320) | copy-start | bytes 26884
  311.1 36.6 %copy-start.215 = (f32[384]{0:T(512)S(1)}, f32[384]{0:T(512)}, u32[]{:S(2)}) copy-start(f32[384]{0:T(512)} %get-tuple-element.339) | copy-start | bytes 4612
  414.8 40.1 %copy-start.105 = (f32[8,384]{1,0:T(8,128)S(1)}, f32[8,384]{1,0:T(8,128)}, u32[]{:S(2)}) copy-start(f32[8,384]{1,0:T(8,128)} %copy-done.104) | copy-start | bytes 36868
  480.6 28.2 %copy-start.166 = (f32[8,384]{1,0:T(8,128)S(1)}, f32[8,384]{1,0:T(8,128)}, u32[]{:S(2)}) copy-start(f32[8,384]{1,0:T(8,128)} %get-tuple-element.253) | copy-start | bytes 36868
  480.6 28.2 %copy-start.167 = (f32[8,384]{1,0:T(8,128)S(1)}, f32[8,384]{1,0:T(8,128)}, u32[]{:S(2)}) copy-start(f32[8,384]{1,0:T(8,128)} %get-tuple-element.254) | copy-start | bytes 36868
  480.6 28.2 %copy-start.168 = (f32[8,384]{1,0:T(8,128)S(1)}, f32[8,384]{1,0:T(8,128)}, u32[]{:S(2)}) copy-start(f32[8,384]{1,0:T(8,128)} %get-tuple-element.255) | copy-start | bytes 36868
  480.6 28.2 %copy-start.169 = (f32[8,384]{1,0:T(8,128)S(1)}, f32[8,384]{1,0:T(8,128)}, u32[]{:S(2)}) copy-start(f32[8,384]{1,0:T(8,128)} %get-tuple-element.256) | copy-start | bytes 36868
  480.6 28.2 %copy-start.170 = (f32[8,384]{1,0:T(8,128)S(1)}, f32[8,384]{1,0:T(8,128)}, u32[]{:S(2)}) copy-start(f32[8,384]{1,0:T(8,128)} %get-tuple-element.257) | copy-start | bytes 36868
  480.6 28.2 %copy-start.171 = (f32[8,384]{1,0:T(8,128)S(1)}, f32[8,384]{1,0:T(8,128)}, u32[]{:S(2)}) copy-start(f32[8,384]{1,0:T(8,128)} %get-tuple-element.258) | copy-start | bytes 36868
  480.6 28.2 %copy-start.172 = (f32[8,384]{1,0:T(8,128)S(1)}, f32[8,384]{1,0:T(8,128)}, u32[]{:S(2)}) copy-start(f32[8,384]{1,0:T(8,128)} %get-tuple-element.259) | copy-start | bytes 36868
  480.7 28.2 %copy-start.173 = (f32[8,384]{1,0:T(8,128)S(1)}, f32[8,384]{1,0:T(8,128)}, u32[]{:S(2)}) copy-start(f32[8,384]{1,0:T(8,128)} %get-tuple-element.260) | copy-start | bytes 36868
  480.7 28.2 %copy-start.174 = (f32[8,384]{1,0:T(8,128)S(1)}, f32[8,384]{1,0:T(8,128)}, u32[]{:S(2)}) copy-start(f32[8,384]{1,0:T(8,128)} %get-tuple-element.261) | copy-start | bytes 36868
  480.7 28.2 %copy-start.175 = (f32[8,384]{1,0:T(8,128)S(1)}, f32[8,384]{1,0:T(8,128)}, u32[]{:S(2)}) copy-start(f32[8,384]{1,0:T(8,128)} %get-tuple-element.262) | copy-start | bytes 36868
  480.7 28.2 %copy-start.176 = (f32[8,384]{1,0:T(8,128)S(1)}, f32[8,384]{1,0:T(8,128)}, u32[]{:S(2)}) copy-start(f32[8,384]{1,0:T(8,128)} %get-tuple-element.263) | copy-start | bytes 36868
  480.7 28.2 %copy-start.177 = (f32[8,384]{1,0:T(8,128)S(1)}, f32[8,384]{1,0:T(8,128)}, u32[]{:S(2)}) copy-start(f32[8,384]{1,0:T(8,128)} %get-tuple-element.264) | copy-start | bytes 36868
  480.7 28.2 %copy-start.178 = (f32[8,384]{1,0:T(8,128)S(1)}, f32[8,384]{1,0:T(8,128)}, u32[]{:S(2)}) copy-start(f32[8,384]{1,0:T(8,128)} %get-tuple-element.265) | copy-start | bytes 36868
  578.5 59.7 %copy-start.1 = (f32[8,14,20,384]{3,2,1,0:T(8,128)S(1)}, f32[8,14,20,384]{3,2,1,0:T(8,128)}, u32[]{:S(2)}) copy-start(f32[8,14,20,384]{3,2,1,0:T(8,128)} %get-tuple-element.355) | copy-start | bytes 10321924
  578.5 59.7 %copy-start.36 = (f32[8,14,20]{2,1,0:T(8,128)S(1)}, f32[8,14,20]{2,1,0:T(8,128)}, u32[]{:S(2)}) copy-start(f32[8,14,20]{2,1,0:T(8,128)} %copy-done.35) | copy-start | bytes 26884
  638.3 46.7 %copy-start.65 = (f32[8,384]{1,0:T(8,128)S(1)}, f32[8,384]{1,0:T(8,128)}, u32[]{:S(2)}) copy-start(f32[8,384]{1,0:T(8,128)} %get-tuple-element.318) | copy-start | bytes 36868
  638.3 46.7 %copy-start.67 = (f32[8,384]{1,0:T(8,128)S(1)}, f32[8,384]{1,0:T(8,128)}, u32[]{:S(2)}) copy-start(f32[8,384]{1,0:T(8,128)} %get-tuple-element.319) | copy-start | bytes 36868
  638.3 46.6 %copy-start.69 = (f32[8,384]{1,0:T(8,128)S(1)}, f32[8,384]{1,0:T(8,128)}, u32[]{:S(2)}) copy-start(f32[8,384]{1,0:T(8,128)} %get-tuple-element.320) | copy-start | bytes 36868
  638.3 46.6 %copy-start.71 = (f32[8,384]{1,0:T(8,128)S(1)}, f32[8,384]{1,0:T(8,128)}, u32[]{:S(2)}) copy-start(f32[8,384]{1,0:T(8,128)} %get-tuple-element.321) | copy-start | bytes 36868
  638.3 46.6 %copy-start.73 = (f32[8,384]{1,0:T(8,128)S(1)}, f32[8,384]{1,0:T(8,128)}, u32[]{:S(2)}) copy-start(f32[8,384]{1,0:T(8,128)} %get-tuple-element.322) | copy-start | bytes 36868
  638.3 46.6 %copy-start.75 = (f32[8,384]{1,0:T(8,128)S(1)}, f32[8,384]{1,0:T(8,128)}, u32[]{:S(2)}) copy-start(f32[8,384]{1,0:T(8,128)} %get-tuple-element.323) | copy-start | bytes 36868
  638.3 46.6 %copy-start.77 = (f32[8,384]{1,0:T(8,128)S(1)}, f32[8,384]{1,0:T(8,128)}, u32[]{:S(2)}) copy-start(f32[8,384]{1,0:T(8,128)} %get-tuple-element.299) | copy-start | bytes 36868
  638.3 46.6 %copy-start.79 = (f32[8,384]{1,0:T(8,128)S(1)}, f32[8,384]{1,0:T(8,128)}, u32[]{:S(2)}) copy-start(f32[8,384]{1,0:T(8,128)} %get-tuple-element.316) | copy-start | bytes 36868
  638.3 46.6 %copy-start.81 = (f32[8,384]{1,0:T(8,128)S(1)}, f32[8,384]{1,0:T(8,128)}, u32[]{:S(2)}) copy-start(f32[8,384]{1,0:T(8,128)} %get-tuple-element.317) | copy-start | bytes 36868
  685.0 27.4 %copy-start.107 = (f32[8,384]{1,0:T(8,128)S(1)}, f32[8,384]{1,0:T(8,128)}, u32[]{:S(2)}) copy-start(f32[8,384]{1,0:T(8,128)} %get-tuple-element.300) | copy-start | bytes 36868
  735.7 28.6 %copy-start.34 = (f32[8,14,20]{2,1,0:T(8,128)S(1)}, f32[8,14,20]{2,1,0:T(8,128)}, u32[]{:S(2)}) copy-start(f32[8,14,20]{2,1,0:T(8,128)} %copy-done.33) | copy-start | bytes 26884
  764.2 33.8 %copy-start.47 = (f32[8,384]{1,0:T(8,128)S(1)}, f32[8,384]{1,0:T(8,128)}, u32[]{:S(2)}) copy-start(f32[8,384]{1,0:T(8,128)} %copy-done.46) | copy-start | bytes 36868
  764.3 33.8 %copy-start.49 = (f32[8,384]{1,0:T(8,128)S(1)}, f32[8,384]{1,0:T(8,128)}, u32[]{:S(2)}) copy-start(f32[8,384]{1,0:T(8,128)} %get-tuple-element.331) | copy-start | bytes 36868
  764.3 33.8 %copy-start.51 = (f32[8,384]{1,0:T(8,128)S(1)}, f32[8,384]{1,0:T(8,128)}, u32[]{:S(2)}) copy-start(f32[8,384]{1,0:T(8,128)} %get-tuple-element.332) | copy-start | bytes 36868
  764.3 33.8 %copy-start.53 = (f32[8,384]{1,0:T(8,128)S(1)}, f32[8,384]{1,0:T(8,128)}, u32[]{:S(2)}) copy-start(f32[8,384]{1,0:T(8,128)} %get-tuple-element.333) | copy-start | bytes 36868
  764.3 33.8 %copy-start.55 = (f32[8,384]{1,0:T(8,128)S(1)}, f32[8,384]{1,0:T(8,128)}, u32[]{:S(2)}) copy-start(f32[8,384]{1,0:T(8,128)} %get-tuple-element.334) | copy-start | bytes 36868
  764.3 33.8 %copy-start.57 = (f32[8,384]{1,0:T(8,128)S(1)}, f32[8,384]{1,0:T(8,128)}, u32[]{:S(2)}) copy-start(f32[8,384]{1,0:T(8,128)} %get-tuple-element.335) | copy-start | bytes 36868
  764.3 33.8 %copy-start.59 = (f32[8,384]{1,0:T(8,128)S(1)}, f32[8,384]{1,0:T(8,128)}, u32[]{:S(2)}) copy-start(f32[8,384]{1,0:T(8,128)} %get-tuple-element.336) | copy-start | bytes 36868
  764.3 33.8 %copy-start.61 = (f32[8,384]{1,0:T(8,128)S(1)}, f32[8,384]{1,0:T(8,128)}, u32[]{:S(2)}) copy-start(f32[8,384]{1,0:T(8,128)} %get-tuple-element.337) | copy-start | bytes 36868
  764.3 33.8 %copy-start.63 = (f32[8,384]{1,0:T(8,128)S(1)}, f32[8,384]{1,0:T(8,128)}, u32[]{:S(2)}) copy-start(f32[8,384]{1,0:T(8,128)} %get-tuple-element.338) | copy-start | bytes 36868
  (184 other events, 2822.8 us)
Sparse Core Ops, SparseCore 0:
  14.2 133.4 all-reduce.186
  150.6 56.9 all-gather.1
  869.2 166.9 all-reduce.184
where the time goes:
time: 1050 us
  other arithmetic  544 us (52%)
  waiting for transfers between devices  261 us (25%)
  matrix products  117 us (11%)
  local copies, waits for them, and re-layouts  108 us (10%)
  between operations  18 us (2%)
    unnamed x5, waiting for transfers between devices  261 us
    reduce_sum x6, other arithmetic, depthwise(): window * kernel[:, row_shift, col_shift][:, None, None, :]  201 us
    add_any x4, other arithmetic, depthwise(): padded[:, row_shift:row_shift + rows_in, col_shift:col_shift + cols_in, :]  103 us
    mul x5, other arithmetic, depthwise(): window * kernel[:, row_shift, col_shift][:, None, None, :]  101 us
    dot_general x5, matrix products, matmul(): return jnp.dot(left, right, preferred_element_type=jnp.float32)  58.3 us
    mul x3, other arithmetic, gelu_exact(): return jax.nn.gelu(values, approximate=False)  52.5 us
    reduce_sum x1, other arithmetic, focal(): summary = gelu_exact(jnp.mean(level_ctx, axis=(1, 2), keepdims=True))  50.3 us
    dot_general x5, matrix products, times_turned(): lax.dot_general(left, right, (((1,), (1,)), ((), ())), preferred_element_...  40.5 us
  transfers between devices with their start and end apart: 3, of which 2 were waited for; matrix products, arithmetic and copies ran while one was open for 18% of the time, Pallas kernels for 0%

commit v1 on v0

v1 whole, which is shorter than its diff:
```python
import functools

import jax
import jax.numpy as jnp
import numpy as np
from jax import lax
from jax.experimental import pallas as pl
from jax.experimental.pallas import tpu as pltpu
from jax.sharding import PartitionSpec as P

C = 384
HID = 1536
GH = 14
GW = 20
HALF = 144
IMG = 2 * HALF
PAIR = 2 * IMG
C2 = 2 * C
NY = 17
NX = 23
NV = 12
NU = 8
Q = NU * NV
AR = 2 * (Q + 16)
BR = 2 * Q
SR = 4 * Q + 32
LEVELS = (3, 5, 7)
TAPS = 64
GATES = 128
MERGED = C2 + GATES
BROWS = 768
HCHUNK = 512
AXES = ("gx", "gy")
f32 = jnp.float32
bf16 = jnp.bfloat16
EPS = 1e-05
ROOT_HALF = 0.7071067811865476
INV_ROOT_2PI = 0.3989422804014327


def _hi(a):
    return a.astype(bf16)


def _lo(a):
    return (a - a.astype(bf16).astype(np.float64)).astype(bf16)


@functools.lru_cache(maxsize=None)
def constants():
    row = np.arange(HALF)
    real = (row < 7 * GW).astype(np.float64)
    yy = np.minimum(row // GW, 6) - (GH - 1) / 2
    xx = row % GW - (GW - 1) / 2
    uv = [(u, v) for u in range(1, NU + 1) for v in range(NV)]
    u0 = [(0, v) for v in range(NV)]
    wu = 2 * np.pi / NY
    wv = 2 * np.pi / NX

    def trig(pairs, pad):
        u = np.array([p[0] for p in pairs] + [0] * pad, np.float64)[:, None]
        v = np.array([p[1] for p in pairs] + [0] * pad, np.float64)[:, None]
        use = np.array([1.0] * len(pairs) + [0.0] * pad)[:, None] * real[None]
        cy, sy = np.cos(wu * u * yy) * use, np.sin(wu * u * yy) * use
        cx, sx = np.cos(wv * v * xx), np.sin(wv * v * xx)
        weight = np.where(u > 0, 2.0, 1.0) * np.where(v > 0, 2.0, 1.0) / (NY * NX)
        return cy * cx, -cy * sx, sy * cx, -sy * sx, weight

    e_re, e_im, o_re, o_im, w1 = trig(uv, 0)
    z_re, z_im, _, _, w0 = trig(u0, 16 - NV)
    fe = np.concatenate([e_re, z_re, e_im, z_im], 0)
    fo = np.concatenate([o_re, o_im], 0)
    half = np.concatenate([0.5 * w1, w0, 0.5 * w1, w0], 0)
    ge = (fe * half).T
    go = (fo * np.concatenate([0.5 * w1, 0.5 * w1], 0)).T

    es, adj = [], []
    for k in LEVELS:
        h = k // 2
        ty, tx = np.meshgrid(np.arange(k) - h, np.arange(k) - h, indexing="ij")
        u = np.array([p[0] for p in uv], np.float64)[:, None]
        v = np.array([p[1] for p in uv], np.float64)[:, None]
        v0 = np.array(list(range(NV)) + [0] * (16 - NV), np.float64)[:, None]
        use0 = np.array([1.0] * NV + [0.0] * (16 - NV))[:, None]
        for bucket in (0, 1):
            sy, sx = (ty, tx) if bucket == 0 else (tx, ty)
            py = sy.reshape(1, -1) * wu
            px = sx.reshape(1, -1) * wv
            plus = u * py + v * px
            minus = -u * py + v * px
            zero = v0 * px
            e = np.concatenate(
                [np.cos(plus), np.sin(plus), np.cos(minus), np.sin(minus), np.cos(zero) * use0, np.sin(zero) * use0], 0
            )
            wp = np.where(v > 0, 2.0, 1.0) / (NY * NX)
            wz = np.where(v0 > 0, 2.0, 1.0) * use0 / (NY * NX)
            a = np.concatenate(
                [
                    np.cos(plus) * wp,
                    -np.sin(plus) * wp,
                    np.cos(minus) * wp,
                    -np.sin(minus) * wp,
                    np.cos(zero) * wz,
                    -np.sin(zero) * wz,
                ],
                0,
            ).T
            full = np.zeros((SR, TAPS))
            full[:, : k * k] = e
            es.append(np.concatenate([_hi(full), _lo(full)], 1))
            back = np.zeros((TAPS, SR))
            back[: k * k] = a
            adj.append(np.concatenate([_hi(back), _hi(back), _lo(back)], 1))
    return dict(
        fe=np.concatenate([_hi(fe), _lo(fe), _hi(fe)], 1),
        fo=np.concatenate([_hi(fo), _lo(fo), _hi(fo)], 1),
        ge=np.concatenate([_hi(ge), _lo(ge), _hi(ge)], 1),
        go=np.concatenate([_hi(go), _lo(go), _hi(go)], 1),
        es=np.stack(es),
        adj=np.stack(adj),
    )


def dot(a, b):
    return jnp.dot(a, b, preferred_element_type=f32)


def dot_nt(a, b):
    return lax.dot_general(a, b, (((1,), (1,)), ((), ())), preferred_element_type=f32)


def dot_tn(a, b):
    return lax.dot_general(a, b, (((0,), (0,)), ((), ())), preferred_element_type=f32)


def gelu_pair(x):
    cdf = 0.5 * lax.erf(x * ROOT_HALF) + 0.5
    return x * cdf, cdf + x * (jnp.exp(x * x * -0.5) * INV_ROOT_2PI)


def split(x):
    hi = x.astype(bf16)
    return hi, (x - hi.astype(f32)).astype(bf16)


def rows16(i, n=16):
    return pl.ds(pl.multiple_of(i * n, n), n)


def at(base, i, n=16):
    return pl.ds(pl.multiple_of(base + i * n, n), n)


def loop(n, body, init=None, unroll=1):
    if init is None:

        def plain(i, c):
            body(i)
            return c

        lax.fori_loop(0, n, plain, 0, unroll=unroll)
        return None
    return lax.fori_loop(0, n, body, init, unroll=unroll)


def norm_stats(x):
    mean = jnp.mean(x, axis=-1, keepdims=True)
    centred = x - mean
    var = jnp.mean(centred * centred, axis=-1, keepdims=True)
    r = lax.rsqrt(var + EPS)
    return centred * r, r


def sum8(x):
    n = x.shape[0] // 8
    total = x[0:8]
    for k in range(1, n):
        total = total + x[8 * k : 8 * k + 8]
    return total


def grid_rows(im, y):
    return im * IMG + (y * GW if y < 7 else HALF + (GH - 1 - y) * GW)


def lanes(im):
    return slice(im * C, im * C + C)


(V_G1, V_B1, V_BQ, V_BC, V_HB, V_PB, V_S1, V_G2, V_B2, V_BM2, V_S2, V_BG) = range(12)
VROWS = 16


def kernel_a(
    bucket, counts, x_ref, cot_ref, wf, wh, wp, vec, kcat, es, fe, fo, ge, go,
    xrow_o, up_o, normed_o, q_o, gates_o, mod_o, mixed_o, modulated_o, branch_o, z_o, g_o, spec_o, mean_o, h_o,
    xr, ctx, ecat, ocat, s_a, s_b, s_e, s_o, yca, ycb, mix,
):
    step = pl.program_id(0)

    @pl.when(step == 0)
    def _():
        xr[...] = jnp.zeros_like(xr)
        for lb in range(6):
            h_o[lb] = dot(es[lb], kcat[lb // 2])

    for im in range(2):
        live = (step * 2 + im < counts[0]).astype(f32)
        for y in range(GH):
            at_row = grid_rows(im, y)
            xr[at_row : at_row + GW, :] = cot_ref[im, y].astype(f32) * live

    def move_up(i):
        s = rows16(i, 32)
        up_o[s, :] = xr[s, :].astype(bf16)

    loop(PAIR // 32, move_up)
    for im in range(2):
        for y in range(GH):
            at_row = grid_rows(im, y)
            xr[at_row : at_row + GW, :] = x_ref[im, y].astype(f32)

    g1, b1 = vec[V_G1 : V_G1 + 1, :], vec[V_B1 : V_B1 + 1, :]

    def norm(i):
        s = rows16(i, 32)
        x = xr[s, :]
        xrow_o[s, :] = x.astype(bf16)
        n, _ = norm_stats(x)
        normed_o[s, :] = (n * g1 + b1).astype(bf16)

    loop(PAIR // 32, norm)
    q_o[...] = dot(normed_o[...], wf[:, :C]) + vec[V_BQ : V_BQ + 1, :]
    ctx[...] = dot(normed_o[...], wf[:, C:C2]) + vec[V_BC : V_BC + 1, :]
    gates_o[...] = dot(normed_o[...], wf[:, C2:]) + vec[V_BG : V_BG + 1, :GATES]

    def put_pair(im, i, top, bot):
        e_hi, e_lo = split(top + bot)
        o_hi, o_lo = split(top - bot)
        for base, ev, ov in ((0, e_hi, o_hi), (HALF, e_hi, o_hi), (2 * HALF, e_lo, o_lo)):
            ecat[at(base, i), lanes(im)] = ev
            ocat[at(base, i), lanes(im)] = ov

    for im in range(2):

        def first(i, im=im):
            put_pair(im, i, ctx[at(im * IMG, i), :], ctx[at(im * IMG + HALF, i), :])

        loop(HALF // 16, first)

    for level in range(3):
        s_a[...] = dot(fe[...], ecat[...])
        s_b[...] = dot(fo[...], ocat[...])
        base = level * SR
        for im in range(2):
            b = bucket[step * 2 + im]
            lb = level * 2 + b
            for lt in range(3):
                ls = slice(im * C + lt * 128, im * C + lt * 128 + 128)
                hs = slice(lt * 128, lt * 128 + 128)

                def filt(i, ls=ls, hs=hs, lb=lb, base=base):
                    a_re, a_im = s_a[at(0, i), ls], s_a[at(Q + 16, i), ls]
                    b_re, b_im = s_b[at(0, i), ls], s_b[at(Q, i), ls]
                    xp_re, xp_im = a_re + b_im, a_im - b_re
                    xm_re, xm_im = a_re - b_im, a_im + b_re
                    spec_o[at(base, i), ls] = xp_re
                    spec_o[at(base + Q, i), ls] = xp_im
                    spec_o[at(base + 2 * Q, i), ls] = xm_re
                    spec_o[at(base + 3 * Q, i), ls] = xm_im
                    p_re, p_im = h_o[lb, at(0, i), hs], h_o[lb, at(Q, i), hs]
                    q_re, q_im = h_o[lb, at(2 * Q, i), hs], h_o[lb, at(3 * Q, i), hs]
                    yp_re, yp_im = p_re * xp_re - p_im * xp_im, p_re * xp_im + p_im * xp_re
                    ym_re, ym_im = q_re * xm_re - q_im * xm_im, q_re * xm_im + q_im * xm_re
                    for dst, off, width, val in (
                        (yca, 0, AR, yp_re + ym_re),
                        (yca, Q + 16, AR, yp_im + ym_im),
                        (ycb, 0, BR, ym_im - yp_im),
                        (ycb, Q, BR, yp_re - ym_re),
                    ):
                        hi, lo = split(val)
                        dst[at(off, i), ls] = hi
                        dst[at(off + width, i), ls] = hi
                        dst[at(off + 2 * width, i), ls] = lo

                loop(Q // 16, filt)
            ls = lanes(im)
            x_re, x_im = s_a[Q : Q + 16, ls], s_a[2 * Q + 16 : 2 * Q + 32, ls]
            spec_o[base + 4 * Q : base + 4 * Q + 16, ls] = x_re
            spec_o[base + 4 * Q + 16 : base + 4 * Q + 32, ls] = x_im
            p_re, p_im = h_o[lb, 4 * Q : 4 * Q + 16, :], h_o[lb, 4 * Q + 16 : 4 * Q + 32, :]
            for off, val in ((Q, p_re * x_re - p_im * x_im), (2 * Q + 16, p_re * x_im + p_im * x_re)):
                hi, lo = split(val)
                yca[off : off + 16, ls] = hi
                yca[off + AR : off + AR + 16, ls] = hi
                yca[off + 2 * AR : off + 2 * AR + 16, ls] = lo
        s_e[...] = dot(ge[...], yca[...])
        s_o[...] = dot(go[...], ycb[...])
        for im in range(2):

            def act(i, total, im=im, level=level):
                ls = lanes(im)
                even, odd = s_e[at(0, i), ls], s_o[at(0, i), ls]
                both = []
                for h, a in ((0, even + odd), (HALF, even - odd)):
                    z, g = gelu_pair(a)
                    z_o[at(level * IMG + h, i), ls] = z.astype(bf16)
                    g_o[at(level * IMG + h, i), ls] = g
                    s = at(im * IMG + h, i)
                    part = z * gates_o[s, level : level + 1]
                    mix[s, :] = part if level == 0 else mix[s, :] + part
                    both.append(z)
                if level < 2:
                    put_pair(im, i, both[0], both[1])
                    return total
                return total + sum8(both[0]) + sum8(both[1])

            total = loop(HALF // 16, act, jnp.zeros((8, C), f32))
            if level == 2:
                mean = jnp.sum(total, axis=0, keepdims=True) * (1.0 / (GH * GW))
                mean_o[:, lanes(im)] = jnp.broadcast_to(mean, (8, C))

    for im in range(2):
        glob, _ = gelu_pair(mean_o[0:1, lanes(im)])

        def finish(i, im=im, glob=glob):
            s = at(im * IMG, i, 32)
            mixed_o[s, :] = (mix[s, :] + gates_o[s, 3:4] * glob).astype(bf16)

        loop(IMG // 32, finish)
    mod_o[...] = dot(mixed_o[...], wh[...]) + vec[V_HB : V_HB + 1, :]

    def modulate(i):
        s = rows16(i, 32)
        modulated_o[s, :] = (q_o[s, :] * mod_o[s, :]).astype(bf16)

    loop(PAIR // 32, modulate)
    branch_o[...] = dot(modulated_o[...], wp[...]) + vec[V_PB : V_PB + 1, :]


(S_S1, S_G2, S_B2, S_BM2, S_S2) = range(5)


def kernel_b(
    x_ref, branch, up, w1, w2, vec, bm1,
    dmid_o, out_o, gw1, gw2, sums, bsum,
    mid, second, dshr, shr, dsec, act, dexp, hid, vacc, bacc,
):
    step = pl.program_id(0)

    @pl.when(step == 0)
    def _():
        gw1[...] = jnp.zeros_like(gw1)
        gw2[...] = jnp.zeros_like(gw2)
        vacc[...] = jnp.zeros_like(vacc)
        bacc[...] = jnp.zeros_like(bacc)

    g2, b2 = vec[V_G2 : V_G2 + 1, :], vec[V_B2 : V_B2 + 1, :]
    s1, s2 = vec[V_S1 : V_S1 + 1, :], vec[V_S2 : V_S2 + 1, :]

    def norm(i):
        s = rows16(i, 32)
        middle = x_ref[s, :].astype(f32) + s1 * branch[s, :]
        mid[s, :] = middle
        n, _ = norm_stats(middle)
        second[s, :] = (n * g2 + b2).astype(bf16)
        dshr[s, :] = (up[s, :].astype(f32) * s2).astype(bf16)

    loop(BROWS // 32, norm)
    for h in range(HID // HCHUNK):
        hs = slice(h * HCHUNK, (h + 1) * HCHUNK)
        hid[...] = dot(second[...], w1[:, hs]) + bm1[0:1, hs]
        dact = dot_nt(dshr[...], w2[hs, :])
        dsec_h = dact
        shr_h = hid
        del dsec_h, shr_h
        act_g = dact

        def gelu(i, hs=hs):
            s = rows16(i, 16)
            z, g = gelu_pair(hid[s, :])
            act[s, :] = z.astype(bf16)
            hid[s, :] = g

        loop(BROWS // 16, gelu)
        d = act_g * hid[...]
        dexp[...] = d.astype(bf16)
        bacc[:, hs] += jnp.sum(d.reshape(BROWS // 8, 8, HCHUNK), axis=0)
        part = dot(act[...], w2[hs, :])
        back = dot_nt(dexp[...], w1[:, hs])
        if h == 0:
            shr[...] = part
            dsec[...] = back
        else:
            shr[...] += part
            dsec[...] += back
        gw1[:, hs] += dot_tn(second[...], dexp[...])
        gw2[hs, :] += dot_tn(act[...], dshr[...])

    bm2 = vec[V_BM2 : V_BM2 + 1, :]

    def finish(i, c):
        t_s1, t_g2, t_b2, t_bm2, t_s2 = c
        s = rows16(i, 32)
        middle = mid[s, :]
        u = up[s, :].astype(f32)
        shrunk = shr[s, :] + bm2
        out_o[s, :] = middle + s2 * shrunk
        n, r = norm_stats(middle)
        d = dsec[s, :]
        e = d * g2
        dn = d * n
        dv = r * (e - jnp.mean(e, axis=-1, keepdims=True) - n * jnp.mean(e * n, axis=-1, keepdims=True))
        dm = u + dv
        dmid_o[s, :] = dm
        return (
            t_s1 + sum8(dm * branch[s, :]),
            t_g2 + sum8(dn),
            t_b2 + sum8(d),
            t_bm2 + sum8(dshr[s, :].astype(f32)),
            t_s2 + sum8(u * shrunk),
        )

    zero = jnp.zeros((8, C), f32)
    totals = loop(BROWS // 32, finish, (zero,) * 5)
    for k, t in enumerate(totals):
        vacc[k] += t

    @pl.when(step == pl.num_programs(0) - 1)
    def _():
        sums[...] = jnp.zeros_like(sums)
        for k in range(5):
            sums[k : k + 1, :] = jnp.sum(vacc[k], axis=0, keepdims=True)
        bsum[...] = jnp.broadcast_to(jnp.sum(bacc[...], axis=0, keepdims=True), bsum.shape)


(T_PB, T_HB, T_G1, T_B1) = range(4)


def kernel_c(
    bucket, counts, dmid, out_rows, x_ref, normed, q_ref, gates, mod, mixed, modulated, z_ref, g_ref, spec, mean_ref, h_ref,
    wf, wh, wp, vec, adj, fe, fo, ge, go,
    gtok_o, out_o, gwf, gwh, gwp, sums, fsum, dk,
    stage, dmix, dmer, d1, d2, ecat, ocat, s_a, s_b, s_e, s_o, yca, ycb, acc, cat, vacc, facc,
):
    step = pl.program_id(0)
    last = pl.num_programs(0) - 1

    @pl.when(step == 0)
    def _():
        for ref in (gwf, gwh, gwp, vacc, facc, acc):
            ref[...] = jnp.zeros_like(ref)

    s1, g1 = vec[V_S1 : V_S1 + 1, :], vec[V_G1 : V_G1 + 1, :]
    zero = jnp.zeros((8, C), f32)

    def scale(i, t):
        s = rows16(i, 32)
        d = s1 * dmid[s, :]
        d1[s, :] = d.astype(bf16)
        return t + sum8(d)

    vacc[T_PB] += loop(PAIR // 32, scale, zero)
    gwp[...] += dot_tn(modulated[...], d1[...])
    dmix[...] = dot_nt(d1[...], wp[...])

    def demod(i, c):
        t_q, t_hb = c
        s = rows16(i, 32)
        dm = dmix[s, :]
        dq = dm * mod[s, :]
        dd = dm * q_ref[s, :]
        dmer[s, :C] = dq.astype(bf16)
        d2[s, :] = dd.astype(bf16)
        return t_q + sum8(dq), t_hb + sum8(dd)

    t_q, t_hb = loop(PAIR // 32, demod, (zero, zero))
    facc[:, :C] += t_q
    vacc[T_HB] += t_hb
    gwh[...] += dot_tn(mixed[...], d2[...])
    dmix[...] = dot_nt(d2[...], wh[...])

    lane = lax.broadcasted_iota(jnp.int32, (16, GATES), 1)
    dmeans = []
    for im in range(2):
        ls = lanes(im)
        glob, dglob = gelu_pair(mean_ref[0:1, ls])

        def gate_grad(i, c, im=im, ls=ls, glob=glob):
            t_glob, t_g = c
            for h in (0, HALF):
                s = at(im * IMG + h, i)
                dm = dmix[s, :]
                dg = jnp.zeros((16, GATES), f32)
                for k in range(4):
                    other = z_ref[at(k * IMG + h, i), ls].astype(f32) if k < 3 else glob
                    col = jnp.sum(dm * other, axis=-1, keepdims=True)
                    dg = jnp.where(lane == k, col, dg)
                dmer[s, C2:] = dg.astype(bf16)
                t_g = t_g + sum8(dg)
                t_glob = t_glob + sum8(dm * gates[s, 3:4])
            return t_glob, t_g

        t_glob, t_g = loop(HALF // 16, gate_grad, (zero, jnp.zeros((8, GATES), f32)))
        facc[:, C2:] += t_g
        dmeans.append(jnp.sum(t_glob, axis=0, keepdims=True) * dglob * (1.0 / (GH * GW)))

    for level in (2, 1, 0):
        for im in range(2):
            ls = lanes(im)

            def before(i, im=im, ls=ls, level=level, dmean=dmeans[im]):
                parts = []
                if level < 2:
                    even, odd = s_e[at(0, i), ls], s_o[at(0, i), ls]
                    through = (even + odd, even - odd)
                else:
                    through = (dmean, dmean)
                for k, h in enumerate((0, HALF)):
                    s = at(im * IMG + h, i)
                    dz = gates[s, level : level + 1] * dmix[s, :] + through[k]
                    parts.append(dz * g_ref[at(level * IMG + h, i), ls])
                ecat[at(0, i), ls] = (parts[0] + parts[1]).astype(bf16)
                ocat[at(0, i), ls] = (parts[0] - parts[1]).astype(bf16)

            loop(HALF // 16, before)
        s_a[...] = dot(fe[...], ecat[...])
        s_b[...] = dot(fo[...], ocat[...])
        base = level * SR
        for im in range(2):
            b = bucket[step * 2 + im]
            lb = level * 2 + b
            for lt in range(3):
                ls = slice(im * C + lt * 128, im * C + lt * 128 + 128)
                hs = slice(lt * 128, lt * 128 + 128)

                def filt(i, ls=ls, hs=hs, lb=lb, base=base):
                    a_re, a_im = s_a[at(0, i), ls], s_a[at(Q + 16, i), ls]
                    b_re, b_im = s_b[at(0, i), ls], s_b[at(Q, i), ls]
                    dp_re, dp_im = a_re + b_im, a_im - b_re
                    dm_re, dm_im = a_re - b_im, a_im + b_re
                    xp_re, xp_im = spec[at(base, i), ls], spec[at(base + Q, i), ls]
                    xm_re, xm_im = spec[at(base + 2 * Q, i), ls], spec[at(base + 3 * Q, i), ls]
                    acc[lb, at(0, i), hs] += xp_re * dp_re + xp_im * dp_im
                    acc[lb, at(Q, i), hs] += xp_im * dp_re - xp_re * dp_im
                    acc[lb, at(2 * Q, i), hs] += xm_re * dm_re + xm_im * dm_im
                    acc[lb, at(3 * Q, i), hs] += xm_im * dm_re - xm_re * dm_im
                    p_re, p_im = h_ref[lb, at(0, i), hs], h_ref[lb, at(Q, i), hs]
                    q_re, q_im = h_ref[lb, at(2 * Q, i), hs], h_ref[lb, at(3 * Q, i), hs]
                    yp_re, yp_im = p_re * dp_re + p_im * dp_im, p_re * dp_im - p_im * dp_re
                    ym_re, ym_im = q_re * dm_re + q_im * dm_im, q_re * dm_im - q_im * dm_re
                    yca[at(0, i), ls] = (yp_re + ym_re).astype(bf16)
                    yca[at(Q + 16, i), ls] = (yp_im + ym_im).astype(bf16)
                    ycb[at(0, i), ls] = (ym_im - yp_im).astype(bf16)
                    ycb[at(Q, i), ls] = (yp_re - ym_re).astype(bf16)

                loop(Q // 16, filt)
            ls = lanes(im)
            d_re, d_im = s_a[Q : Q + 16, ls], s_a[2 * Q + 16 : 2 * Q + 32, ls]
            x_re = spec[base + 4 * Q : base + 4 * Q + 16, ls]
            x_im = spec[base + 4 * Q + 16 : base + 4 * Q + 32, ls]
            acc[lb, 4 * Q : 4 * Q + 16, :] += x_re * d_re + x_im * d_im
            acc[lb, 4 * Q + 16 : 4 * Q + 32, :] += x_im * d_re - x_re * d_im
            p_re, p_im = h_ref[lb, 4 * Q : 4 * Q + 16, :], h_ref[lb, 4 * Q + 16 : 4 * Q + 32, :]
            yca[Q : Q + 16, ls] = (p_re * d_re + p_im * d_im).astype(bf16)
            yca[2 * Q + 16 : 2 * Q + 32, ls] = (p_re * d_im - p_im * d_re).astype(bf16)
        s_e[...] = dot(ge[...], yca[...])
        s_o[...] = dot(go[...], ycb[...])

    for im in range(2):
        ls = lanes(im)

        def context(i, t, im=im, ls=ls):
            even, odd = s_e[at(0, i), ls], s_o[at(0, i), ls]
            top, bot = even + odd, even - odd
            dmer[at(im * IMG, i), C:C2] = top.astype(bf16)
            dmer[at(im * IMG + HALF, i), C:C2] = bot.astype(bf16)
            return t + sum8(top) + sum8(bot)

        facc[:, C:C2] += loop(HALF // 16, context, zero)

    gwf[...] += dot_tn(normed[...], dmer[...])
    dmix[...] = dot_nt(dmer[...], wf[...])

    def norm_back(i, c):
        t_g, t_b = c
        s = rows16(i, 32)
        n, r = norm_stats(x_ref[s, :].astype(f32))
        d = dmix[s, :]
        e = d * g1
        dv = r * (e - jnp.mean(e, axis=-1, keepdims=True) - n * jnp.mean(e * n, axis=-1, keepdims=True))
        stage[s, :] = dmid[s, :] + dv
        return t_g + sum8(d * n), t_b + sum8(d)

    t_g, t_b = loop(PAIR // 32, norm_back, (zero, zero))
    vacc[T_G1] += t_g
    vacc[T_B1] += t_b
    for im in range(2):
        live = (step * 2 + im < counts[0]).astype(f32)
        for y in range(GH):
            at_row = grid_rows(im, y)
            gtok_o[im, y] = stage[at_row : at_row + GW, :]
            out_o[im, y] = (out_rows[at_row : at_row + GW, :] * live).astype(bf16)

    @pl.when(step == last)
    def _():
        sums[...] = jnp.zeros_like(sums)
        for k in range(4):
            sums[k : k + 1, :] = jnp.sum(vacc[k], axis=0, keepdims=True)
        fsum[...] = jnp.broadcast_to(jnp.sum(facc[...], axis=0, keepdims=True), fsum.shape)
        for level in range(3):
            total = None
            for b in range(2):
                lb = level * 2 + b

                def parts(i, lb=lb):
                    hi, lo = split(acc[lb, at(0, i), :])
                    cat[at(0, i), :] = hi
                    cat[at(SR, i), :] = lo
                    cat[at(2 * SR, i), :] = hi

                loop(SR // 16, parts)
                term = dot(adj[lb], cat[...])
                total = term if total is None else total + term
            dk[level] = total


def full(shape):
    return pl.BlockSpec(shape, lambda i, n=len(shape): (0,) * n)


def rows(n, width):
    return pl.BlockSpec((n, width), lambda i: (i, 0))


def smem():
    return pl.BlockSpec(memory_space=pltpu.SMEM)


def image_block():
    return pl.BlockSpec((2, GH, GW, C), lambda i: (i, 0, 0, 0))


def sds(shape, dtype):
    return jax.ShapeDtypeStruct(shape, dtype)


def params(mib):
    return pltpu.CompilerParams(vmem_limit_bytes=mib * 2**20, dimension_semantics=("arbitrary",))


def compute(tokens, bucket, counts, wf, wh, wp, w1, w2, vec, bm1, kcat, cotangent):
    con = constants()
    slots = tokens.shape[0]
    pairs = slots // 2
    n = pairs * PAIR
    fwd = [jnp.asarray(con[k]) for k in ("fe", "fo", "ge", "go")]
    a_out = [
        (sds((n, C), bf16), rows(PAIR, C)),
        (sds((n, C), bf16), rows(PAIR, C)),
        (sds((n, C), bf16), rows(PAIR, C)),
        (sds((n, C), f32), rows(PAIR, C)),
        (sds((n, GATES), f32), rows(PAIR, GATES)),
        (sds((n, C), f32), rows(PAIR, C)),
        (sds((n, C), bf16), rows(PAIR, C)),
        (sds((n, C), bf16), rows(PAIR, C)),
        (sds((n, C), f32), rows(PAIR, C)),
        (sds((pairs * 3 * IMG, C2), bf16), rows(3 * IMG, C2)),
        (sds((pairs * 3 * IMG, C2), f32), rows(3 * IMG, C2)),
        (sds((pairs * 3 * SR, C2), f32), rows(3 * SR, C2)),
        (sds((pairs * 8, C2), f32), rows(8, C2)),
        (sds((6, SR, C), f32), full((6, SR, C))),
    ]
    xrow, up, normed, q, gates, mod, mixed, modulated, branch, z, g, spec, mean, h = pl.pallas_call(
        kernel_a,
        grid=(pairs,),
        out_shape=[o[0] for o in a_out],
        out_specs=[o[1] for o in a_out],
        in_specs=[smem(), smem(), image_block(), image_block()]
        + [full(w.shape) for w in (wf, wh, wp, vec, kcat, con["es"], *fwd)],
        scratch_shapes=[
            pltpu.VMEM((PAIR, C), f32),
            pltpu.VMEM((PAIR, C), f32),
            pltpu.VMEM((3 * HALF, C2), bf16),
            pltpu.VMEM((3 * HALF, C2), bf16),
            pltpu.VMEM((AR, C2), f32),
            pltpu.VMEM((BR, C2), f32),
            pltpu.VMEM((HALF, C2), f32),
            pltpu.VMEM((HALF, C2), f32),
            pltpu.VMEM((3 * AR, C2), bf16),
            pltpu.VMEM((3 * BR, C2), bf16),
            pltpu.VMEM((PAIR, C), f32),
        ],
        compiler_params=params(60),
        name="focal_forward",
    )(bucket, counts, tokens, cotangent, wf, wh, wp, vec, kcat, jnp.asarray(con["es"]), *fwd)

    b_out = [
        (sds((n, C), f32), rows(BROWS, C)),
        (sds((n, C), f32), rows(BROWS, C)),
        (sds((C, HID), f32), full((C, HID))),
        (sds((HID, C), f32), full((HID, C))),
        (sds((8, C), f32), full((8, C))),
        (sds((8, HID), f32), full((8, HID))),
    ]
    dmid, out_rows, gw1, gw2, sums_b, bsum = pl.pallas_call(
        kernel_b,
        grid=(n // BROWS,),
        out_shape=[o[0] for o in b_out],
        out_specs=[o[1] for o in b_out],
        in_specs=[rows(BROWS, C)] * 3 + [full(w.shape) for w in (w1, w2, vec, bm1)],
        scratch_shapes=[
            pltpu.VMEM((BROWS, C), f32),
            pltpu.VMEM((BROWS, C), bf16),
            pltpu.VMEM((BROWS, C), bf16),
            pltpu.VMEM((BROWS, C), f32),
            pltpu.VMEM((BROWS, C), f32),
            pltpu.VMEM((BROWS, HCHUNK), bf16),
            pltpu.VMEM((BROWS, HCHUNK), bf16),
            pltpu.VMEM((BROWS, HCHUNK), f32),
            pltpu.VMEM((5, 8, C), f32),
            pltpu.VMEM((8, HID), f32),
        ],
        compiler_params=params(60),
        name="mlp",
    )(xrow, branch, up, w1, w2, vec, bm1)

    bwd = [jnp.asarray(con["fe"][:, :HALF]), jnp.asarray(con["fo"][:, :HALF])]
    bwd += [jnp.asarray(con["ge"][:, :AR]), jnp.asarray(con["go"][:, :BR])]
    c_out = [
        (sds(tokens.shape, f32), image_block()),
        (sds(tokens.shape, bf16), image_block()),
        (sds((C, MERGED), f32), full((C, MERGED))),
        (sds((C, C), f32), full((C, C))),
        (sds((C, C), f32), full((C, C))),
        (sds((8, C), f32), full((8, C))),
        (sds((8, MERGED), f32), full((8, MERGED))),
        (sds((3, TAPS, C), f32), full((3, TAPS, C))),
    ]
    gtok, out, gwf, gwh, gwp, sums_c, fsum, dk = pl.pallas_call(
        kernel_c,
        grid=(pairs,),
        out_shape=[o[0] for o in c_out],
        out_specs=[o[1] for o in c_out],
        in_specs=[smem(), smem()]
        + [rows(PAIR, C)] * 5
        + [rows(PAIR, GATES)]
        + [rows(PAIR, C)] * 3
        + [rows(3 * IMG, C2)] * 2
        + [rows(3 * SR, C2), rows(8, C2), full(h.shape)]
        + [full(w.shape) for w in (wf, wh, wp, vec, con["adj"], *bwd)],
        scratch_shapes=[
            pltpu.VMEM((PAIR, C), f32),
            pltpu.VMEM((PAIR, C), f32),
            pltpu.VMEM((PAIR, MERGED), bf16),
            pltpu.VMEM((PAIR, C), bf16),
            pltpu.VMEM((PAIR, C), bf16),
            pltpu.VMEM((HALF, C2), bf16),
            pltpu.VMEM((HALF, C2), bf16),
            pltpu.VMEM((AR, C2), f32),
            pltpu.VMEM((BR, C2), f32),
            pltpu.VMEM((HALF, C2), f32),
            pltpu.VMEM((HALF, C2), f32),
            pltpu.VMEM((AR, C2), bf16),
            pltpu.VMEM((BR, C2), bf16),
            pltpu.VMEM((6, SR, C), f32),
            pltpu.VMEM((3 * SR, C), bf16),
            pltpu.VMEM((4, 8, C), f32),
            pltpu.VMEM((8, MERGED), f32),
        ],
        compiler_params=params(62),
        name="focal_backward",
    )(
        bucket, counts, dmid, out_rows, xrow, normed, q, gates, mod, mixed, modulated, z, g, spec, mean, h,
        wf, wh, wp, vec, jnp.asarray(con["adj"]), *bwd,
    )
    return out, gtok, gwf, gwh, gwp, gw1, gw2, sums_b, bsum, sums_c, fsum, dk


def unpack_weights(mod_full, mlp_full, small):
    cut = C * (C2 + 4)
    wf = jnp.pad(mod_full[:cut].reshape(C, C2 + 4), ((0, 0), (0, GATES - 4)))
    wh = mod_full[cut : cut + C * C].reshape(C, C)
    wp = mod_full[cut + C * C :].reshape(C, C)
    w1 = mlp_full[: C * HID].reshape(C, HID)
    w2 = mlp_full[C * HID :].reshape(HID, C)
    k0 = 4 * C + 4
    taps = small[k0 : k0 + 83 * C].reshape(83, C)
    kc = []
    start = 0
    for k in LEVELS:
        piece = jnp.pad(taps[start : start + k * k], ((0, TAPS - k * k), (0, 0)))
        kc.append(jnp.concatenate([piece, piece], 0))
        start += k * k
    kcat = jnp.stack(kc)
    s32 = small.astype(f32)
    tail = k0 + 83 * C

    def seg(offset):
        return s32[offset : offset + C]

    order = [seg(0), seg(C), seg(2 * C), seg(3 * C), seg(tail), seg(tail + C), seg(tail + 2 * C), seg(tail + 3 * C), seg(tail + 4 * C)]
    order += [seg(tail + 5 * C + HID), seg(tail + 6 * C + HID), jnp.pad(s32[4 * C : 4 * C + 4], (0, C - 4))]
    vec = jnp.pad(jnp.stack(order), ((0, VROWS - len(order)), (0, 0)))
    bm1 = jnp.broadcast_to(s32[None, tail + 5 * C : tail + 5 * C + HID], (8, HID))
    return wf, wh, wp, w1, w2, vec, bm1, kcat


def pack_small(sums_b, bsum, sums_c, fsum, dk, size):
    flat = [
        sums_c[T_G1], sums_c[T_B1], fsum[0, : C2 + 4], dk[0, :9].reshape(-1), dk[1, :25].reshape(-1), dk[2, :49].reshape(-1),
        sums_c[T_HB], sums_c[T_PB], sums_b[S_S1], sums_b[S_G2], sums_b[S_B2], bsum[0], sums_b[S_BM2], sums_b[S_S2],
    ]
    used = 94 * C + 4 + HID
    return jnp.concatenate(flat + [jnp.zeros((size - used,), f32)])


def local(tokens, bucket, counts, mod_weights, mlp_weights, small_params, cotangent):
    mod_full = lax.all_gather(mod_weights, AXES, axis=0, tiled=True)
    small = lax.all_gather(small_params, AXES, axis=0, tiled=True)
    mlp_full = lax.all_gather(mlp_weights, AXES, axis=0, tiled=True)
    wf, wh, wp, w1, w2, vec, bm1, kcat = unpack_weights(mod_full, mlp_full, small)
    out, gtok, gwf, gwh, gwp, gw1, gw2, sums_b, bsum, sums_c, fsum, dk = compute(
        tokens, bucket, counts, wf, wh, wp, w1, w2, vec, bm1, kcat, cotangent
    )
    mlp_flat = jnp.concatenate([gw1.reshape(-1), gw2.reshape(-1)])
    grad_mlp = lax.psum_scatter(mlp_flat, AXES, scatter_dimension=0, tiled=True)
    mod_flat = jnp.concatenate([gwf[:, : C2 + 4].reshape(-1), gwh.reshape(-1), gwp.reshape(-1)])
    small_flat = pack_small(sums_b, bsum, sums_c, fsum, dk, small.shape[0])
    grad_mod = lax.psum_scatter(mod_flat, AXES, scatter_dimension=0, tiled=True)
    grad_small = lax.psum_scatter(small_flat, AXES, scatter_dimension=0, tiled=True)
    return out, gtok, grad_mod, grad_mlp, grad_small


def solution(mesh):
    images = P(AXES, None, None, None)
    flat = P(AXES)
    return jax.shard_map(
        local,
        mesh=mesh,
        in_specs=(images, flat, flat, flat, flat, flat, images),
        out_specs=(images, images, flat, flat, flat),
        check_vma=False,
    )
```

time: 1050 us -> 614 us (0.58)
  other arithmetic: 544 us -> 6.41 us
  Pallas kernels: 0 us -> 241 us
  matrix products: 117 us -> 0 us
  local copies, waits for them, and re-layouts: 108 us -> 56.6 us
  waiting for transfers between devices: 261 us -> 294 us
    reduce_sum x18 -> x0, other arithmetic: 268 us -> none  [the longest x6 201 us: depthwise(): window * kernel[:, row_shift, col_shift][:, None, None, :]]
    pallas_call x0 -> x3, Pallas kernels: none -> 241 us  [the longest x1 92.2 us: compute(): pl.pallas_call(kernel_c, grid=(pairs,), out_shape=[o[0] for o in c_out],...]
    mul x8 -> x0, other arithmetic: 154 us -> none  [the longest x5 101 us: depthwise(): window * kernel[:, row_shift, col_shift][:, None, None, :]]
    dot_general x15 -> x0, matrix products: 117 us -> none  [the longest x5 58.3 us: matmul(): return jnp.dot(left, right, preferred_element_type=jnp.float32)]
    add_any x8 -> x0, other arithmetic: 103 us -> none  [the longest x4 103 us: depthwise(): padded[:, row_shift:row_shift + rows_in, col_shift:col_shift + cols_in, :]]
    unnamed x5, waiting for transfers between devices: 261 us -> 294 us
    convert_element_type x9 -> x0, local copies, waits for them, and re-layouts: 23.3 us -> none  [the longest x2 7.06 us: local(): upstream = cotangent.reshape(-1, C).astype(jnp.float32) * rows_alive]
    reshape x20 -> x6, local copies, waits for them, and re-layouts: 29.9 us -> 13.2 us  [the longest x2 5.58 us: local(): mlp_flat = jnp.concatenate([gw1.reshape(-1), gw2.reshape(-1)])]
  transfers between devices with their start and end apart: 3 -> 3, of which waited for: 2 -> 2; matrix products, arithmetic and copies ran while one was open for 18% -> 4% of each run, Pallas kernels for 0% -> 13%
where the time goes in v1:
time: 614 us; the launch traced here: 613 us
  waiting for transfers between devices  294 us (48%)
  Pallas kernels  241 us (39%)
  local copies, waits for them, and re-layouts  56.6 us (9%)
  between operations  15 us (2%)
  other arithmetic  6.41 us (1%)
    unnamed x5, waiting for transfers between devices  294 us
    pallas_call x1, Pallas kernels, compute(): pl.pallas_call(kernel_c, grid=(pairs,), out_shape=[o[0] for o in c_out],...  92.2 us
    pallas_call x1, Pallas kernels, compute(): pl.pallas_call(kernel_a, grid=(pairs,), out_shape=[o[0] for o in a_out],...  76.9 us
    pallas_call x1, Pallas kernels, compute(): pl.pallas_call(kernel_b, grid=(n // BROWS,), out_shape=[o[0] for o in b_o...  71.7 us
    unnamed x53, local copies, waits for them, and re-layouts  17.6 us
  transfers between devices with their start and end apart: 3, of which 2 were waited for; matrix products, arithmetic and copies ran while one was open for 4% of the time, Pallas kernels for 13%

profile of v1, /device:TPU:0, one launch (start us, length us, event | category | flops | bytes accessed | tf_op | source)
XLA Modules:
  0.0 612.6 jit_solution(9310817024801618096)
XLA Ops:
  7.3 1.3 dynamic-update-slice
  8.6 0.9 dynamic-update-slice.1
  10.3 0.7 all-gather.2.cloned.1.call-update
  11.8 1.6 copy.30.x_ref
  13.4 1.6 copy.31.cot_ref
  15.0 132.6 %all-reduce.18.cloned.1.call-done = (bf16[37664]{0:T(1024)(128)(2,1)}, bf16[591360]{0:T(1024)(128)(2,1)}) async-done(((bf16[37664]{0:T(1024)(128)(2,1)}, bf16[591360]{0:T(1024)(128)(2,1)}), (bf16[37664]{0:T(1024)(128)(2,1)}, bf16[591360]{0:T(1024)(128)(2,1)})) %all-reduce.18.cloned.1.call-update) | async-done | bytes 1258064
  147.7 0.7 slice.224
  148.3 0.8 slice.226
  149.1 0.8 slice.225
  149.9 0.9 slice.227
  150.8 0.8 slice.230
  151.6 0.9 fusion.2
  153.4 1.1 slice.210
  154.5 1.2 fusion.1
  155.7 0.8 slice.169.wh
  156.6 0.9 slice.171.wp
  157.4 1.5 reshape.75
  158.9 0.9 pad.24.wf
  159.9 0.8 pad_maximum_fusion.2.kcat
  160.6 76.9 %focal_forward.1 = (bf16[2304,384]{1,0:T(8,128)(2,1)}, bf16[2304,384]{1,0:T(8,128)(2,1)}, bf16[2304,384]{1,0:T(8,128)(2,1)}, f32[2304,384]{1,0:T(8,128)}, f32[23...) custom-call(s32[8]{0:T(128)} %bucket.3, ...), custom_call_target="tpu_custom_call" | custom-call | tf_op jit(solution)/shard_map/focal_forward/pallas_call | solution.py:674
  237.6 1.8 fusion
  239.4 2.2 slice.191.w1
  241.5 1.4 slice.193.w2
  242.9 0.6 broadcast_in_dim.2.bm1
  243.6 71.7 %mlp.1 = (f32[2304,384]{1,0:T(8,128)}, f32[2304,384]{1,0:T(8,128)}, f32[384,1536]{1,0:T(8,128)}, f32[1536,384]{1,0:T(8,128)}, f32[8,384]{1,0:T(8,128)}, /*index=5*/f32[8,1536]{1,0:T(8,128)}) custom-call(bf16[2304,384]{1,0:T(8,128)(2,1)} %get-tuple-element.33.x_ref, f32[2304,384]{1,0:T(8,128)} %get-tuple-element.34.branch, ...), custom_call_target="tpu_custom_call" | custom-call | tf_op jit(solution)/shard_map/mlp/pallas_call | solution.py:706
  315.3 92.2 %focal_backward.1 = (f32[8,14,20,384]{3,2,1,0:T(8,128)}, bf16[8,14,20,384]{3,2,1,0:T(8,128)(2,1)}, f32[384,896]{1,0:T(8,128)}, f32[384,384]{1,0:T(8,128)}, f32[3...) custom-call(s32[8]{0:T(128)} %bucket.3, s32[1]{0:T(128)S(6)} %copy.41.counts, ...), custom_call_target="tpu_custom_call" | custom-call | tf_op jit(solution)/shard_map/focal_backward/pallas_call | solution.py:740
  407.5 0.9 slice.201
  408.3 0.8 slice.200
  409.1 0.7 slice.199
  409.9 0.6 reshape_squeeze.11
  411.8 1.5 slice_reduce_fusion.7
  413.2 1.4 slice_reduce_fusion.1
  414.6 0.6 slice_reduce_fusion.2
  415.2 0.8 slice_reduce_fusion
  416.0 2.3 reshape.79
  418.4 3.2 reshape.80
  421.6 2.3 reshape.76
  423.9 1.9 reshape.77
  425.8 1.9 reshape.78
  427.7 4.1 pad_maximum_fusion
  432.0 1.5 pad_maximum_fusion.1
  433.6 0.8 concatenate.23
  434.4 5.2 copy.33
  439.6 1.6 copy.32
  441.2 160.3 %all-reduce.16.cloned.1.call-done = (f32[591360]{0:T(1024)}, f32[1179648]{0:T(1024)}, f32[37664]{0:T(1024)}) async-done(((f32[591360]{0:T(1024)}, f32[1179648]{0:T(1024)}, f32[37664]{0:T(1024)}), (f32[591360]{0:T(1024)}, f32[1179648]{0:T(1024)}, f32[37664]{0:T(1024)})) %all-reduce.16.cloned.1.call-update) | async-done | bytes 7234704
  601.5 1.6 dynamic-slice.1
  603.0 1.6 dynamic-slice
  604.7 1.4 dynamic-slice.2
  (76 shorter events, 3.0 us)
Async XLA Ops:
  7.2 4.7 copy-start.4
  7.2 140.5 %all-reduce.18.cloned.1.call-start = ((), (), s32[]{:S(2)}) async-start(), calls=%async_computation.2 | async-start | bytes 2519040
  8.6 1.0 copy-start
  9.6 0.6 copy-start.7
  10.2 227.3 %all-gather.2.cloned.1.call-start = ((), (), s32[]{:S(2)}) async-start(), calls=%async_computation | async-start | bytes 2433024 | tf_op jit(solution)/shard_map/all_gather | solution.py:821
  11.0 590.5 %all-reduce.16.cloned.1.call-start = ((), (), s32[]{:S(2)}) async-start(), calls=%async_computation.1 | async-start | bytes 14475264
  11.0 2.4 copy-start.5
  315.3 99.3 %copy-start.20 = (f32[8,384]{1,0:T(8,128)S(1)}, f32[8,384]{1,0:T(8,128)}, u32[]{:S(2)}) copy-start(f32[8,384]{1,0:T(8,128)} %get-tuple-element.59) | copy-start | bytes 36868
  427.7 4.1 copy-start.1
  427.7 4.1 copy-start.2
  431.8 1.7 copy-start.6
  431.8 1.7 copy-start.8
  431.9 1.7 copy-start.9
  431.9 1.7 copy-start.10
  431.9 1.7 copy-start.11
  431.9 1.7 copy-start.12
  431.9 1.7 copy-start.13
  431.9 1.7 copy-start.14
  431.9 1.7 copy-start.15
  431.9 1.7 copy-start.16
  431.9 1.7 copy-start.17
  431.9 1.7 copy-start.18
  432.0 1.7 copy-start.19
  434.4 5.2 copy-start.3
Sparse Core Ops, SparseCore 0:
  14.2 133.4 all-reduce.17
  150.6 57.1 all-gather.1
  434.5 166.8 all-reduce.15
